TPU v7x, 128 devices: a whole 4x4x4 slice. The times are simulated.
128 devices in a mesh: section: 16 (over y, x_lo, core), peer: 8 (over x_hi, z).
Axes of the slice: x: 4 (x_hi: 2, x_lo: 2; x = x_hi * 2 + x_lo), y: 4, z: 4, core: 2. Of those that a mesh axis runs over, the one named last changes fastest.
Arguments:
- inputs: bfloat16 [16, 8, 128, 2560], P('section', 'peer'), may hold values from -6 to 6
- wiring: int32 [2, 16, 8], replicated, may hold values from 0 to 7, as said below
- lengths: int32 [16, 8], replicated, may hold values from 16 to 128
- norm_gain: bfloat16 [16, 2560], P('section'), may hold values from 0.25 to 1.75
- w_query: bfloat16 [16, 2560, 3072], P('section', None, 'peer'), may hold values from -0.5 to 0.5
- w_key: bfloat16 [16, 2560, 3072], P('section', None, 'peer'), may hold values from -0.5 to 0.5
- w_value: bfloat16 [16, 2560, 3072], P('section', None, 'peer'), may hold values from -0.125 to 0.125
- w_out: bfloat16 [16, 3072, 2560], P('section', 'peer'), may hold values from -0.109375 to 0.109375
- cotangent: bfloat16 [16, 8, 128, 2560], P('section', 'peer'), may hold values from -0.59765625 to 0.59765625
Outputs:
- final_out: bfloat16 [16, 8, 128, 2560], P('section', 'peer')
- input_grad: bfloat16 [16, 8, 128, 2560], P('section', 'peer')
- gain_grad: float32 [16, 2560], P('section')
- w_query_grad: bfloat16 [16, 2560, 3072], P('section', None, 'peer')
- w_key_grad: bfloat16 [16, 2560, 3072], P('section', None, 'peer')
- w_value_grad: bfloat16 [16, 2560, 3072], P('section', None, 'peer')
- w_out_grad: bfloat16 [16, 3072, 2560], P('section', 'peer')
Inputs may be any that keep to these rules, and one draw needn't show every extreme that they name: Each wiring[h, s, :] is a permutation of the peers 0 to 7.
All inputs are finite; a program needn't handle non-finite values.
Results may differ from a plain program's by a relative error of at most 0.022.
The roundings to bfloat16 on the way count: a program that leaves them out, or rounds other values in their place, can miss the bound.
Values may be sent and summed in bfloat16 or wider, within the bound.
No kernel may reach another device: no remote copies, remote signals or barrier semaphores. Data moves between devices by JAX's collectives and lax.ppermute only.
A program may use at most 192 MiB of HBM per device.

v0:
```python
import math

import jax
import jax.numpy as jnp
from jax import lax
from jax.sharding import PartitionSpec as P

HD = 128


eps = 1e-05


def shifted(value, axis, by):
    size = lax.axis_size(axis)
    return lax.ppermute(value, axis, [(i, (i + by) % size) for i in range(size)])


def invert(permutation):
    peer_count = permutation.shape[-1]
    numbers = jnp.arange(peer_count, dtype=jnp.int32)
    matches = permutation[..., None, :] == numbers[:, None]
    return jnp.sum(jnp.where(matches, numbers, 0), axis=-1)


def lookup(table_rows, positions):
    peer_count = table_rows.shape[-1]
    numbers = jnp.arange(peer_count, dtype=jnp.int32)
    matches = positions[..., :, None] == numbers
    return jnp.sum(jnp.where(matches, table_rows[..., None, :], 0), axis=-1)


def probabilities(query_heads, key_heads, seq_lengths):
    seq_rows = query_heads.shape[1]
    score_scale = 1.0 / math.sqrt(query_heads.shape[3])
    scores = (
        jnp.einsum("mihc,mjhc->mhij", query_heads, key_heads, preferred_element_type=jnp.float32)
        * score_scale
    )
    positions = jnp.arange(seq_rows, dtype=jnp.int32)
    allowed = (positions[None, :, None] >= positions[None, None, :]) & (
        positions[None, None, :] < seq_lengths[:, None, None]
    )
    scores = jnp.where(allowed[:, None], scores, -1e30)
    row_max = jnp.max(scores, axis=-1, keepdims=True)
    exp_scores = jnp.exp(scores - row_max)
    return exp_scores / jnp.sum(exp_scores, axis=-1, keepdims=True)


def per_device(inputs, wiring, lengths, norm_gain, w_query, w_key, w_value, w_out, cotangent):
    section_count = lax.axis_size("section")
    section_index = lax.axis_index("section")
    peer_index = lax.axis_index("peer")
    prev_section = (section_index + section_count - 1) % section_count
    first_map = lax.dynamic_index_in_dim(wiring[0], prev_section, 0, keepdims=False)
    second_map = lax.dynamic_index_in_dim(wiring[1], section_index, 0, keepdims=False)
    onward = lookup(second_map, first_map)
    sender_of = invert(onward)
    seq_lengths = lax.dynamic_index_in_dim(lengths, prev_section, 0, keepdims=False)
    grouped = lax.all_gather(inputs, "peer", axis=1, tiled=True)
    gathered = shifted(grouped, "section", 1)
    grouped_back = lax.all_gather(cotangent, "peer", axis=1, tiled=True)
    later = shifted(grouped_back, "section", -1)
    entering = gathered[0]
    d_out = jnp.take(later[0], onward, axis=0)
    batches, seq_rows, model_width = entering.shape
    inner_local = w_query.shape[2]
    local_heads = inner_local // HD
    score_scale = 1.0 / math.sqrt(HD)
    gain_full = norm_gain[0].astype(jnp.float32)
    wq_local = w_query[0]
    wk_local = w_key[0]
    wv_local = w_value[0]
    wo_local = w_out[0]
    act_full = entering.astype(jnp.float32)
    inv_rms = lax.rsqrt(jnp.mean(act_full * act_full, axis=-1, keepdims=True) + eps)
    unit_rows = act_full * inv_rms
    normed = (unit_rows * gain_full).astype(jnp.bfloat16).reshape(batches * seq_rows, model_width)

    def project(weight_mat):
        product = jnp.dot(normed, weight_mat, preferred_element_type=jnp.float32)
        return product.astype(jnp.bfloat16).reshape(batches, seq_rows, local_heads, HD)

    query_heads = project(wq_local)
    key_heads = project(wk_local)
    value_heads = project(wv_local)
    attn_probs = probabilities(query_heads, key_heads, seq_lengths)
    probs_low = attn_probs.astype(jnp.bfloat16)
    mixed = jnp.einsum(
        "mhij,mjhc->mihc", probs_low, value_heads, preferred_element_type=jnp.float32
    )
    mixed = mixed.astype(jnp.bfloat16)
    mixed_taken = jnp.take(mixed, sender_of, axis=0)
    mixed = mixed.reshape(batches * seq_rows, inner_local)
    mixed_sent = mixed_taken.reshape(batches * seq_rows, inner_local)
    summed = lax.psum_scatter(
        jnp.dot(mixed_sent, wo_local, preferred_element_type=jnp.float32).astype(jnp.bfloat16),
        "peer",
        scatter_dimension=0,
        tiled=True,
    ).astype(jnp.float32)
    own_source = lax.dynamic_index_in_dim(sender_of, peer_index, 0, keepdims=False)
    own_entering = lax.dynamic_index_in_dim(act_full, own_source, 0, keepdims=False)
    layer_out = (own_entering + summed).astype(jnp.bfloat16)
    final_out = shifted(layer_out[None, None], "section", 1)
    grad_rows = d_out.reshape(batches * seq_rows, model_width)
    d_mixed = jnp.dot(grad_rows, wo_local.T, preferred_element_type=jnp.float32).astype(
        jnp.bfloat16
    )
    w_out_grad = jnp.dot(mixed.T, grad_rows, preferred_element_type=jnp.float32).astype(
        jnp.bfloat16
    )
    d_mixed = d_mixed.reshape(batches, seq_rows, local_heads, HD)
    soft_back = probabilities(query_heads, key_heads, seq_lengths)
    soft_low = soft_back.astype(jnp.bfloat16)
    d_values = jnp.einsum(
        "mhij,mihc->mjhc", soft_low, d_mixed, preferred_element_type=jnp.float32
    ).astype(jnp.bfloat16)
    d_probs = jnp.einsum(
        "mihc,mjhc->mhij", d_mixed, value_heads, preferred_element_type=jnp.float32
    )
    row_delta = jnp.sum(soft_back * d_probs, axis=-1, keepdims=True)
    d_scores = (soft_back * (d_probs - row_delta) * score_scale).astype(jnp.bfloat16)
    d_query = jnp.einsum(
        "mhij,mjhc->mihc", d_scores, key_heads, preferred_element_type=jnp.float32
    ).astype(jnp.bfloat16)
    d_keys = jnp.einsum(
        "mhij,mihc->mjhc", d_scores, query_heads, preferred_element_type=jnp.float32
    ).astype(jnp.bfloat16)
    flat_q = d_query.reshape(batches * seq_rows, inner_local)
    flat_k = d_keys.reshape(batches * seq_rows, inner_local)
    flat_v = d_values.reshape(batches * seq_rows, inner_local)
    w_query_grad = jnp.dot(normed.T, flat_q, preferred_element_type=jnp.float32).astype(
        jnp.bfloat16
    )
    w_key_grad = jnp.dot(normed.T, flat_k, preferred_element_type=jnp.float32).astype(jnp.bfloat16)
    w_value_grad = jnp.dot(normed.T, flat_v, preferred_element_type=jnp.float32).astype(
        jnp.bfloat16
    )
    result = jnp.dot(flat_q, wq_local.T, preferred_element_type=jnp.float32)
    result = result + jnp.dot(flat_k, wk_local.T, preferred_element_type=jnp.float32)
    d_normed = lax.psum_scatter(
        (result + jnp.dot(flat_v, wv_local.T, preferred_element_type=jnp.float32)).astype(
            jnp.bfloat16
        ),
        "peer",
        scatter_dimension=0,
        tiled=True,
    ).astype(jnp.float32)
    own_unit = lax.dynamic_index_in_dim(unit_rows, peer_index, 0, keepdims=False)
    own_rms = lax.dynamic_index_in_dim(inv_rms, peer_index, 0, keepdims=False)
    own_grad = lax.dynamic_index_in_dim(d_out, peer_index, 0, keepdims=False)
    gain_part = jnp.sum(d_normed * own_unit, axis=0)
    gain_grad = lax.psum(gain_part, "peer")
    scaled = d_normed * gain_full
    d_act = own_rms * (scaled - own_unit * jnp.mean(scaled * own_unit, axis=-1, keepdims=True))
    d_entering = (own_grad.astype(jnp.float32) + d_act).astype(jnp.bfloat16)
    input_grad = shifted(d_entering[None, None], "section", -1)
    return (
        final_out,
        input_grad,
        gain_grad[None],
        w_query_grad[None],
        w_key_grad[None],
        w_value_grad[None],
        w_out_grad[None],
    )


def solution(mesh):
    return jax.shard_map(
        per_device,
        mesh=mesh,
        in_specs=(
            P("section", "peer", None, None),
            P(),
            P(),
            P("section", None),
            P("section", None, "peer"),
            P("section", None, "peer"),
            P("section", None, "peer"),
            P("section", "peer", None),
            P("section", "peer", None, None),
        ),
        out_specs=(
            P("section", "peer", None, None),
            P("section", "peer", None, None),
            P("section", None),
            P("section", None, "peer"),
            P("section", None, "peer"),
            P("section", None, "peer"),
            P("section", "peer", None),
        ),
        check_vma=False,
    )
```

profile of v0, /device:TPU:4, one launch (start us, length us, event | category | flops | bytes accessed | tf_op | source)
XLA Modules:
  0.0 572.3 jit_solution(17042351142583534226)
XLA Ops:
  8.7 81.9 %all-gather.5.cloned.1.call-done = bf16[1,8,128,2560]{3,2,0,1:T(8,128)(2,1)} async-done(((bf16[1,1,128,2560]{3,2,0,1:T(8,128)(2,1)}), bf16[1,8,128,2560]{3,2,0,1:T(8,128)(2,1)}) %all-gather.5.cloned.1.call-update) | async-done | bytes 5242896 | tf_op jit(solution)/shard_map/all_gather | solution.py:62
  90.6 3.3 collective-permute-start.2
  93.9 95.0 %all-gather.3.cloned.1.call-done = bf16[1,8,128,2560]{3,2,0,1:T(8,128)(2,1)} async-done(((bf16[1,1,128,2560]{3,2,0,1:T(8,128)(2,1)}), bf16[1,8,128,2560]{3,2,0,1:T(8,128)(2,1)}) %all-gather.3.cloned.1.call-update) | async-done | bytes 5242896 | tf_op jit(solution)/shard_map/all_gather | solution.py:60
  192.6 5.7 gather_fusion.1
  198.3 3.2 broadcast_select_fusion
  203.8 3.8 fusion.48
  207.6 2.4 reshape.370
  211.3 39.2 %collective-permute-done = bf16[1,8,128,2560]{3,2,0,1:T(8,128)(2,1)} collective-permute-done((bf16[1,8,128,2560]{3,2,0,1:T(8,128)(2,1)}, bf16[1,8,128,2560]{3,2,0,1:T(8,128)(2,1)}, u32[]{:S(2)}, u32[]{:S(2)}) %collective-permute-start) | collective-permute-done | bytes 5242912 | tf_op jit(solution)/shard_map/ppermute | solution.py:16
  250.5 3.6 multiply_reduce_fusion
  254.0 3.7 multiply_convert_fusion
  260.1 3.8 fusion.45
  267.5 6.9 %fusion.42 = bf16[1024,384]{1,0:T(8,128)(2,1)} fusion(bf16[1024,2560]{1,0:T(8,128)(2,1)} %bitcast.150, bf16[1,2560,384]{2,1,0:T(8,128)(2,1)} %param.13), kind=kOutput, calls=%fused_computation.49 | convolution fusion | flops 2013659136 | bytes 7995392 | tf_op jit(solution)/shard_map/dot_general | solution.py:81
  278.0 6.0 %fusion.39 = bf16[1024,384]{1,0:T(8,128)(2,1)S(1)} fusion(bf16[1024,2560]{1,0:T(8,128)(2,1)} %bitcast.151, bf16[1,2560,384]{2,1,0:T(8,128)(2,1)} %param.15), kind=kOutput, calls=%fused_computation.48 | convolution fusion | flops 2013659136 | bytes 7995392 | tf_op jit(solution)/shard_map/dot_general | solution.py:81
  291.5 2.7 fusion.59
  294.2 3.8 fusion.63
  298.0 4.4 fusion.60
  306.2 5.5 fusion.9
  311.7 6.7 %fusion.13 = f32[1024,2560]{1,0:T(8,128)} fusion(bf16[1,2560,384]{2,1,0:T(8,128)(2,1)S(1)} %copy-done.16, bf16[48,8,8,128]{3,2,1,0:T(8,128)(2,1)S(1)} %bitcast.159), kind=kOutput, calls=%fused_computation.25 | convolution fusion | flops 2013265920 | bytes 13238272 | tf_op jit(solution)/shard_map/dot_general | solution.py:140
  319.4 7.9 %add_convert_fusion = bf16[1024,2560]{1,0:T(8,128)(2,1)} fusion(f32[1024,2560]{1,0:T(8,128)} %fusion.13, f32[1024,2560]{1,0:T(8,128)S(1)} %copy-done.2, bf16[1,2560,384]{2,1,0:T(8,128)(2,1)} %param.15, bf16[48,8,8,128]{3,2,1,0:T(8,128)(2,1)S(1)} %bitcast.162), kind=kOutput, calls=%fused_computation.4 | convolution fusion | flops 2021130240 | bytes 28966912 | tf_op jit(solution)/shard_map/dot_general | solution.py:143
  328.5 2.6 fusion.58
  333.4 4.8 convolution_convert_fusion
  340.8 7.1 %fusion.4 = bf16[1,2560,384]{2,1,0:T(8,128)(2,1)} fusion(bf16[1024,2560]{1,0:T(8,128)(2,1)} %bitcast.152, bf16[48,8,8,128]{3,2,1,0:T(8,128)(2,1)} %bitcast.161), kind=kOutput, calls=%fused_computation.16 | convolution fusion | flops 2014248960 | bytes 7995392 | tf_op jit(solution)/shard_map/dot_general | solution.py:137
  347.9 4.1 fusion.2
  352.0 12.8 %convert_bitcast_fusion = (f32[8,128,2560]{2,1,0:T(8,128)}, f32[1,8,128,2560]{3,2,0,1:T(8,128)}) fusion(bf16[1,8,128,2560]{3,2,0,1:T(8,128)(2,1)} %collective-permute-done), kind=kLoop, calls=%fused_computation.8 | loop fusion | flops 2621440 | bytes 26214400 | tf_op jit(solution)/shard_map/convert_element_type | solution.py:75
  364.9 49.7 %reduce-scatter.5.cloned.1.call-done = bf16[128,2560]{1,0:T(8,128)(2,1)} async-done(((bf16[1024,2560]{1,0:T(8,128)(2,1)}), bf16[128,2560]{1,0:T(8,128)(2,1)}) %reduce-scatter.5.cloned.1.call-update) | async-done | bytes 655376 | tf_op jit(solution)/shard_map/reduce_scatter | solution.py:142
  416.6 2.9 fusion.85
  419.5 3.1 collective-permute-start.3
  422.6 85.7 %reduce-scatter.3.cloned.1.call-done = bf16[128,2560]{1,0:T(8,128)(2,1)} async-done(((bf16[1024,2560]{1,0:T(8,128)(2,1)}), bf16[128,2560]{1,0:T(8,128)(2,1)}) %reduce-scatter.3.cloned.1.call-update) | async-done | bytes 655376 | tf_op jit(solution)/shard_map/reduce_scatter | solution.py:96
  508.3 2.6 fusion.84
  511.1 6.8 %fusion.3 = bf16[1,2560,384]{2,1,0:T(8,128)(2,1)} fusion(bf16[1024,2560]{1,0:T(8,128)(2,1)} %bitcast.153, bf16[48,8,8,128]{3,2,1,0:T(8,128)(2,1)S(1)} %bitcast.158), kind=kOutput, calls=%fused_computation.15 | convolution fusion | flops 2014248960 | bytes 7995392 | tf_op jit(solution)/shard_map/dot_general | solution.py:136
  518.5 3.5 fusion.5
  522.0 41.9 %psum.7 = f32[1,2560]{1,0:T(1,128)} all-reduce(f32[1,2560]{1,0:T(1,128)S(1)} %broadcast_in_dim.113), channel_id=1, replica_groups=mesh['section'=16,'peer'=8] {'peer'}, use_global_device_ids=true, to_apply=%region_10.11 | all-reduce | flops 2560 | bytes 20480 | tf_op jit(solution)/shard_map/psum | solution.py:154
  (109 shorter events, 39.0 us)
Async XLA Ops:
  7.2 252.9 %copy-start = (bf16[1,2560,384]{2,1,0:T(8,128)(2,1)S(1)}, bf16[1,2560,384]{2,1,0:T(8,128)(2,1)}, u32[]{:S(2)}) copy-start(bf16[1,2560,384]{2,1,0:T(8,128)(2,1)} %param.14) | copy-start | bytes 5898244
  7.2 83.4 %all-gather.5.cloned.1.call-start = ((), (), s32[]{:S(2)}) async-start(), calls=%async_computation.4 | async-start | bytes 5898240 | tf_op jit(solution)/shard_map/all_gather | solution.py:62
  7.9 180.9 %all-gather.3.cloned.1.call-start = ((), (), s32[]{:S(2)}) async-start(), calls=%async_computation.2 | async-start | bytes 5898240 | tf_op jit(solution)/shard_map/all_gather | solution.py:60
  8.7 405.9 %reduce-scatter.5.cloned.1.call-start = ((), (), s32[]{:S(2)}) async-start(), calls=%async_computation.5 | async-start | bytes 5898240 | tf_op jit(solution)/shard_map/reduce_scatter | solution.py:142
  90.6 102.0 %collective-permute-start.2 = (bf16[1,8,128,2560]{3,2,0,1:T(8,128)(2,1)}, bf16[1,8,128,2560]{3,2,0,1:T(8,128)(2,1)}, u32[]{:S(2)}, u32[]{:S(2)}) collective-permute-start(bf16[1,8,128,2560]{3,2,0,1:T(8,128)(2,1)} %all-gather.5.cloned.1.call-done), channel_id=1, source_target_pairs={{0,120},{8,0},{16,8},{24,16},{32,24},{40,32},{48,40},{56,48},{64,5... | collective-permute-start | bytes 15728648 | tf_op jit(solution)/shard_map/ppermute | solution.py:16
  188.9 61.6 %collective-permute-start = (bf16[1,8,128,2560]{3,2,0,1:T(8,128)(2,1)}, bf16[1,8,128,2560]{3,2,0,1:T(8,128)(2,1)}, u32[]{:S(2)}, u32[]{:S(2)}) collective-permute-start(bf16[1,8,128,2560]{3,2,0,1:T(8,128)(2,1)} %all-gather.3.cloned.1.call-done), channel_id=1, source_target_pairs={{0,8},{8,16},{16,24},{24,32},{32,40},{40,48},{48,56},{56,64},{64,7... | collective-permute-start | bytes 15728648 | tf_op jit(solution)/shard_map/ppermute | solution.py:16
  190.8 7.5 %copy-start.21 = (s32[8]{0:T(128)}, s32[8]{0:T(128)S(1)}, u32[]{:S(2)}) copy-start(s32[8]{0:T(128)S(1)} %select_reduce_fusion.1) | copy-start | bytes 100
  198.3 5.5 copy-start.19
  201.5 2.3 copy-start.3
  257.8 2.3 copy-start.5
  287.3 4.1 copy-start.4
  287.3 2.1 copy-start.6
  287.4 2.6 copy-start.12
  294.2 3.8 copy-start.13
  302.5 2.3 copy-start.17
  304.2 7.4 %copy-start.8 = (bf16[8,128,3,128]{1,0,3,2:T(8,128)(2,1)}, bf16[8,128,3,128]{1,0,3,2:T(8,128)(2,1)S(1)}, u32[]{:S(2)}) copy-start(bf16[8,128,3,128]{1,0,3,2:T(8,128)(2,1)S(1)} %copy.90) | copy-start | bytes 2359300
  304.8 6.9 %copy-start.10 = (bf16[8,128,3,128]{1,0,3,2:T(8,128)(2,1)}, bf16[8,128,3,128]{1,0,3,2:T(8,128)(2,1)S(1)}, u32[]{:S(2)}) copy-start(bf16[8,128,3,128]{1,0,3,2:T(8,128)(2,1)S(1)} %copy.87) | copy-start | bytes 2359300
  306.2 5.5 copy-start.16
  311.6 7.3 %copy-start.2 = (f32[1024,2560]{1,0:T(8,128)S(1)}, f32[1024,2560]{1,0:T(8,128)}, u32[]{:S(2)}) copy-start(f32[1024,2560]{1,0:T(8,128)} %fusion.9) | copy-start | bytes 31457284
  311.6 7.7 %copy-start.14 = (bf16[8,128,3,128]{1,0,3,2:T(8,128)(2,1)S(1)}, bf16[8,128,3,128]{1,0,3,2:T(8,128)(2,1)}, u32[]{:S(2)}) copy-start(bf16[8,128,3,128]{1,0,3,2:T(8,128)(2,1)} %copy.93) | copy-start | bytes 2359300
  327.3 181.0 %reduce-scatter.3.cloned.1.call-start = ((), (), s32[]{:S(2)}) async-start(), calls=%async_computation.3 | async-start | bytes 5898240 | tf_op jit(solution)/shard_map/reduce_scatter | solution.py:96
  331.8 1.5 copy-start.20
  338.2 9.7 %slice-start.2 = ((s8[5242880]{0:T(1024)(128)(4,1)}), s8[1048576]{0:T(1024)(128)(4,1)S(1)}, s32[]{:S(2)}) async-start(s8[5242880]{0:T(1024)(128)(4,1)} %bitcast.154), calls=%async_computation.8 | async-start | bytes 2097152
  340.8 7.1 %slice-start.3 = ((s8[5242880]{0:T(1024)(128)(4,1)}), s8[4194304]{0:T(1024)(128)(4,1)S(1)}, s32[]{:S(2)}) async-start(s8[5242880]{0:T(1024)(128)(4,1)} %bitcast.154), calls=%async_computation.9 | async-start | bytes 8388608
  340.8 7.1 %copy-start.11 = (bf16[8,128,3,128]{1,0,3,2:T(8,128)(2,1)S(1)}, bf16[8,128,3,128]{1,0,3,2:T(8,128)(2,1)}, u32[]{:S(2)}) copy-start(bf16[8,128,3,128]{1,0,3,2:T(8,128)(2,1)} %copy-done.10) | copy-start | bytes 2359300
  414.5 2.0 copy-start.15
  419.5 91.6 %copy-start.9 = (bf16[8,128,3,128]{1,0,3,2:T(8,128)(2,1)S(1)}, bf16[8,128,3,128]{1,0,3,2:T(8,128)(2,1)}, u32[]{:S(2)}) copy-start(bf16[8,128,3,128]{1,0,3,2:T(8,128)(2,1)} %copy-done.8) | copy-start | bytes 2359300
  419.5 144.4 %collective-permute-start.3 = (bf16[1,1,128,2560]{3,2,1,0:T(8,128)(2,1)}, bf16[1,1,128,2560]{3,2,1,0:T(8,128)(2,1)S(1)}, u32[]{:S(2)}, u32[]{:S(2)}) collective-permute-start(bf16[1,1,128,2560]{3,2,1,0:T(8,128)(2,1)} %fusion.85), channel_id=1, source_target_pairs={{0,120},{8,0},{16,8},{24,16},{32,24},{40,32},{48,40},{56,48},{64,5... | collective-permute-start | bytes 1966088 | tf_op jit(solution)/shard_map/ppermute | solution.py:16
  508.3 10.1 %slice-start = ((s8[5242880]{0:T(1024)(128)(4,1)}), s8[4194304]{0:T(1024)(128)(4,1)S(1)}, s32[]{:S(2)}) async-start(s8[5242880]{0:T(1024)(128)(4,1)} %bitcast.146), calls=%async_computation.6 | async-start | bytes 8388608
  510.9 7.5 %slice-start.1 = ((s8[5242880]{0:T(1024)(128)(4,1)}), s8[1048576]{0:T(1024)(128)(4,1)S(1)}, s32[]{:S(2)}) async-start(s8[5242880]{0:T(1024)(128)(4,1)} %bitcast.146), calls=%async_computation.7 | async-start | bytes 2097152
  510.9 53.0 %collective-permute-start.1 = (bf16[1,1,128,2560]{3,2,1,0:T(8,128)(2,1)}, bf16[1,1,128,2560]{3,2,1,0:T(8,128)(2,1)S(1)}, u32[]{:S(2)}, u32[]{:S(2)}) collective-permute-start(bf16[1,1,128,2560]{3,2,1,0:T(8,128)(2,1)} %fusion.84), channel_id=1, source_target_pairs={{0,8},{8,16},{16,24},{24,32},{32,40},{40,48},{48,56},{56,64},{64,7... | collective-permute-start | bytes 1966088 | tf_op jit(solution)/shard_map/ppermute | solution.py:16
  518.5 47.1 %copy-start.1 = (bf16[1,2560,384]{2,1,0:T(8,128)(2,1)S(1)}, bf16[1,2560,384]{2,1,0:T(8,128)(2,1)}, u32[]{:S(2)}) copy-start(bf16[1,2560,384]{2,1,0:T(8,128)(2,1)} %param.14) | copy-start | bytes 5898244
  (3 other events, 3.1 us)
Sparse Core Ops, SparseCore 0:
  10.3 80.2 all-gather.4
  92.9 95.9 all-gather.2
  327.4 87.0 reduce-scatter.4
  418.2 90.0 reduce-scatter.2
where the time goes:
time: 582 us; the launch traced here: 572 us
  waiting for transfers between devices  353 us (61%)
  matrix products  83.6 us (14%)
  blocking collectives  41.9 us (7%)
  local copies, waits for them, and re-layouts  35.7 us (6%)
  other arithmetic  35.2 us (6%)
  between operations  16.3 us (3%)
  starting transfers between devices  6.77 us (1%)
    all_gather x1, waiting for transfers between devices, per_device(): grouped = lax.all_gather(inputs, 'peer', axis=1, tiled=True)  95 us
    reduce_scatter x1, waiting for transfers between devices, per_device(): lax.psum_scatter(jnp.dot(mixed_sent, wo_local, preferred_element_type=jnp...  85.7 us
    all_gather x1, waiting for transfers between devices, per_device(): grouped_back = lax.all_gather(cotangent, 'peer', axis=1, tiled=True)  81.9 us
    reduce_scatter x1, waiting for transfers between devices, per_device(): lax.psum_scatter((result + jnp.dot(flat_v, wv_local.T, preferred_element_...  49.7 us
    psum x1, blocking collectives, per_device(): gain_grad = lax.psum(gain_part, 'peer')  41.9 us
    ppermute x4, waiting for transfers between devices, shifted(): lax.ppermute(value, axis, [(i, (i + by) % size) for i in range(size)])  39.2 us
    dot_general x3, matrix products, project(): product = jnp.dot(normed, weight_mat, preferred_element_type=jnp.float32)  16.6 us
    convert_element_type x1, other arithmetic, per_device(): act_full = entering.astype(jnp.float32)  12.8 us
  transfers between devices with their start and end apart: 8, of which 5 were waited for; matrix products, arithmetic and copies ran while one was open for 13% of the time, Pallas kernels for 0%

commit v1 on v0

v1 whole, which is shorter than its diff:
```python
import functools
import math

import jax
import jax.numpy as jnp
from jax import lax
from jax.experimental import pallas as pl
from jax.experimental.pallas import tpu as pltpu
from jax.sharding import PartitionSpec as P

HD = 128
TOK = 128
HALF = TOK // 2
HEADS = 3
LOCAL = HEADS * HD
D = 2560
SECTIONS = 16
RING = 4
SCALE = 1.0 / math.sqrt(HD)
eps = 1e-05

F32 = jnp.float32
BF16 = jnp.bfloat16
VMEM_LIMIT = 48 * 1024 * 1024


def moved(value, by_section, flip, by_ring):
    pairs = []
    for section in range(SECTIONS):
        for side in range(2):
            for place in range(RING):
                source = (section * 2 + side) * RING + place
                target = ((section + by_section) % SECTIONS * 2 + (side ^ flip)) * RING
                pairs.append((source, target + (place + by_ring) % RING))
    return lax.ppermute(value, ("section", "peer"), pairs)


def gather_all(own, by):
    held = {}
    held[0] = moved(own, by, 0, 0)
    held[1] = moved(own, by, 1, 0)
    held[6] = moved(own, by, 0, 1)
    held[2] = moved(own, by, 0, -1)
    held[7] = moved(held[1], 0, 0, 1)
    held[3] = moved(held[1], 0, 0, -1)
    parts = [(held[r], 0, r) for r in (0, 1, 2, 6, 3, 7)]
    for dx in range(2):
        parts.append((moved(held[6 + dx][:HALF], 0, 0, 1), 0, 4 + dx))
        parts.append((moved(held[2 + dx][HALF:], 0, 0, -1), HALF, 4 + dx))
    return parts


WHERE = [(0, 0, TOK), (1, 0, TOK), (2, 0, TOK), (6, 0, TOK), (3, 0, TOK), (7, 0, TOK)] + [
    (4, 0, HALF),
    (4, HALF, HALF),
    (5, 0, HALF),
    (5, HALF, HALF),
]


def nt(a, b):
    return lax.dot_general(a, b, (((1,), (1,)), ((), ())), preferred_element_type=F32)


def tn(a, b):
    return lax.dot_general(a, b, (((0,), (0,)), ((), ())), preferred_element_type=F32)


def nn(a, b):
    return jnp.dot(a, b, preferred_element_type=F32)


def load_all(refs, target, sems):
    copies = []
    for k, (number, row, rows) in enumerate(WHERE):
        copies.append(
            pltpu.make_async_copy(refs[k], target.at[number, pl.ds(row, rows)], sems.at[k])
        )
    for copy in copies:
        copy.start()
    for copy in copies:
        copy.wait()


def load_one(refs, wanted, target, sems):
    for k, (number, row, rows) in enumerate(WHERE):

        @pl.when(wanted == number)
        def _(k=k, row=row, rows=rows):
            copy = pltpu.make_async_copy(refs[k], target.at[pl.ds(row, rows)], sems.at[k])
            copy.start()
            copy.wait()


def forward_kernel(
    ids, wiring, lengths, gain, wq, wk, wv, *rest
):
    parts = rest[:10]
    sigma, normed, qkv, probs, mixed, entering, sems = rest[10:]
    section, side, place = ids[0], ids[1], ids[2]
    before = lax.rem(section + SECTIONS - 1, SECTIONS)

    def absolute(r):
        dz, dx = r // 2, r % 2
        return lax.rem(side + dx, 2) * RING + lax.rem(place + dz, RING)

    for r in range(8):
        slot = absolute(r)
        found = jnp.int32(0)
        for m in range(8):
            goes_to = wiring[1, section, wiring[0, before, absolute(m)]]
            found = found + jnp.where(goes_to == slot, m, 0)
        sigma[r] = found

    load_all(parts, entering, sems)
    gain_row = gain[...].astype(F32)

    def norm_one(r, carry):
        act = entering[r].astype(F32)
        inv_rms = lax.rsqrt(jnp.mean(act * act, axis=-1, keepdims=True) + eps)
        normed[r] = (act * inv_rms * gain_row).astype(BF16)
        return carry

    lax.fori_loop(0, 8, norm_one, 0)

    def project(j, carry):
        rows = normed[pl.ds(2 * j, 2)].reshape(2 * TOK, D)
        for c, w in enumerate((wq, wk, wv)):
            out = nn(rows, w[0]).astype(BF16).reshape(2, TOK, LOCAL)
            qkv[pl.ds(2 * j, 2), :, c * LOCAL : (c + 1) * LOCAL] = out
        return carry

    lax.fori_loop(0, 4, project, 0)

    row = lax.broadcasted_iota(jnp.int32, (TOK, TOK), 0)
    col = lax.broadcasted_iota(jnp.int32, (TOK, TOK), 1)

    def attend(r, carry):
        seq_len = lengths[before, absolute(r)]
        allowed = (row >= col) & (col < seq_len)
        for h in range(HEADS):
            q = qkv[r, :, h * HD : (h + 1) * HD]
            k = qkv[r, :, LOCAL + h * HD : LOCAL + (h + 1) * HD]
            v = qkv[r, :, 2 * LOCAL + h * HD : 2 * LOCAL + (h + 1) * HD]
            scores = jnp.where(allowed, nt(q, k) * SCALE, -1e30)
            exp_scores = jnp.exp(scores - jnp.max(scores, axis=-1, keepdims=True))
            p = exp_scores / jnp.sum(exp_scores, axis=-1, keepdims=True)
            probs[r, h] = p
            mixed[r, :, h * HD : (h + 1) * HD] = nn(p.astype(BF16), v).astype(BF16)
        return carry

    lax.fori_loop(0, 8, attend, 0)


ANY = pl.BlockSpec(memory_space=pl.ANY)
SMEM = pl.BlockSpec(memory_space=pltpu.SMEM)
VMEM = pl.BlockSpec(memory_space=pltpu.VMEM)


def params(**more):
    return pltpu.CompilerParams(vmem_limit_bytes=VMEM_LIMIT, **more)


def cost(flops, moved_bytes):
    return pl.CostEstimate(flops=int(flops), bytes_accessed=int(moved_bytes), transcendentals=0)


def forward(ids, wiring, lengths, gain, wq, wk, wv, parts):
    return pl.pallas_call(
        forward_kernel,
        out_shape=(
            jax.ShapeDtypeStruct((8,), jnp.int32),
            jax.ShapeDtypeStruct((8, TOK, D), BF16),
            jax.ShapeDtypeStruct((8, TOK, 3 * LOCAL), BF16),
            jax.ShapeDtypeStruct((8, HEADS, TOK, TOK), F32),
            jax.ShapeDtypeStruct((8, TOK, LOCAL), BF16),
        ),
        in_specs=[SMEM] * 3 + [VMEM] * 4 + [ANY] * 10,
        out_specs=(SMEM, VMEM, VMEM, VMEM, VMEM),
        scratch_shapes=[pltpu.VMEM((8, TOK, D), BF16), pltpu.SemaphoreType.DMA((10,))],
        compiler_params=params(),
        cost_estimate=cost(6.3e9, 20e6),
        name="forward",
    )(ids, wiring, lengths, gain, wq, wk, wv, *parts)


PIECES = {
    "u_up": (4, 0, HALF),
    "u_down": (4, HALF, HALF),
    "v_up": (2, HALF, HALF),
    "v_down": (6, 0, HALF),
    "k_up": (2, 0, HALF),
    "k_down": (6, HALF, HALF),
    "own": (0, 0, TOK),
}
TILE = 512


def store_pieces(outs, total):
    for out, (number, row, rows) in zip(outs, PIECES.values(), strict=True):
        out[...] = total[number : number + 2, row : row + rows].astype(BF16)


def piece_shapes():
    return tuple(jax.ShapeDtypeStruct((2, rows, D), BF16) for _, _, rows in PIECES.values())


def piece_specs():
    return tuple(pl.BlockSpec((2, rows, TILE), lambda n: (0, 0, n)) for _, _, rows in PIECES.values())


def outward_kernel(sigma, mixed, wo, *rest):
    parts = rest[:10]
    outs = rest[10:17]
    sent = rest[17]
    entering, sems = rest[18:]
    tile = pl.program_id(0)

    @pl.when(tile == 0)
    def _():
        for r in range(8):
            sent[r] = mixed[sigma[r]]
        load_one(parts, sigma[0], entering, sems)

    total = nn(sent[...].reshape(8 * TOK, LOCAL), wo[0]).reshape(8, TOK, TILE)
    for out, (number, row, rows) in zip(outs[:6], list(PIECES.values())[:6], strict=True):
        out[...] = total[number : number + 2, row : row + rows].astype(BF16)
    residual = entering[:, pl.ds(pl.multiple_of(tile * TILE, TILE), TILE)].astype(F32)
    outs[6][0] = (total[0] + residual).astype(BF16)
    outs[6][1] = total[1].astype(BF16)


def outward(sigma, mixed, wo, parts):
    whole = lambda *shape: pl.BlockSpec(shape, lambda n: (0,) * len(shape))
    return pl.pallas_call(
        outward_kernel,
        grid=(D // TILE,),
        out_shape=piece_shapes() + (jax.ShapeDtypeStruct((8, TOK, LOCAL), BF16),),
        in_specs=[SMEM, whole(8, TOK, LOCAL), pl.BlockSpec((1, LOCAL, TILE), lambda n: (0, 0, n))]
        + [ANY] * 10,
        out_specs=piece_specs() + (whole(8, TOK, LOCAL),),
        scratch_shapes=[pltpu.VMEM((TOK, D), BF16), pltpu.SemaphoreType.DMA((10,))],
        compiler_params=params(),
        cost_estimate=cost(2e9, 9e6),
        name="outward",
    )(sigma, mixed, wo, *parts)


def back_kernel(sigma, wo, qkv, probs, *rest):
    parts = rest[:10]
    dqkv, grads, d_mixed, sems = rest[10:]
    load_all(parts, grads, sems)

    def project(j, carry):
        rows = grads[pl.ds(2 * j, 2)].reshape(2 * TOK, D)
        d_mixed[pl.ds(2 * j, 2)] = nt(rows, wo[0]).astype(BF16).reshape(2, TOK, LOCAL)
        return carry

    lax.fori_loop(0, 4, project, 0)

    def attend(r, carry):
        m = sigma[r]
        for h in range(HEADS):
            cq = slice(h * HD, (h + 1) * HD)
            ck = slice(LOCAL + h * HD, LOCAL + (h + 1) * HD)
            cv = slice(2 * LOCAL + h * HD, 2 * LOCAL + (h + 1) * HD)
            d = d_mixed[r, :, cq]
            p = probs[m, h]
            dqkv[m, :, cv] = tn(p.astype(BF16), d).astype(BF16)
            d_probs = nt(d, qkv[m, :, cv])
            delta = jnp.sum(p * d_probs, axis=-1, keepdims=True)
            d_scores = (p * (d_probs - delta) * SCALE).astype(BF16)
            dqkv[m, :, cq] = nn(d_scores, qkv[m, :, ck]).astype(BF16)
            dqkv[m, :, ck] = tn(d_scores, qkv[m, :, cq]).astype(BF16)
        return carry

    lax.fori_loop(0, 8, attend, 0)


def back(sigma, wo, qkv, probs, parts):
    return pl.pallas_call(
        back_kernel,
        out_shape=jax.ShapeDtypeStruct((8, TOK, 3 * LOCAL), BF16),
        in_specs=[SMEM] + [VMEM] * 3 + [ANY] * 10,
        out_specs=VMEM,
        scratch_shapes=[
            pltpu.VMEM((8, TOK, D), BF16),
            pltpu.VMEM((8, TOK, LOCAL), BF16),
            pltpu.SemaphoreType.DMA((10,)),
        ],
        compiler_params=params(),
        cost_estimate=cost(3e9, 14e6),
        name="back",
    )(sigma, wo, qkv, probs, *parts)


def inward_kernel(dqkv, wq, wk, wv, normed, gain, *rest):
    outs, gain_part = rest[:7], rest[7]
    flat = dqkv[...].reshape(8 * TOK, 3 * LOCAL)
    total = nt(flat[:, :LOCAL], wq[0])
    total = total + nt(flat[:, LOCAL : 2 * LOCAL], wk[0])
    total = total + nt(flat[:, 2 * LOCAL :], wv[0])
    rows = normed[...].reshape(8 * TOK, TILE).astype(F32)
    gain_part[...] = jnp.sum(total * rows, axis=0, keepdims=True) / gain[...].astype(F32)
    store_pieces(outs, total.reshape(8, TOK, TILE))


def inward(dqkv, wq, wk, wv, normed, gain):
    weight = pl.BlockSpec((1, TILE, LOCAL), lambda n: (0, n, 0))
    line = pl.BlockSpec((1, TILE), lambda n: (0, n))
    return pl.pallas_call(
        inward_kernel,
        grid=(D // TILE,),
        out_shape=piece_shapes() + (jax.ShapeDtypeStruct((1, D), F32),),
        in_specs=[
            pl.BlockSpec((8, TOK, 3 * LOCAL), lambda n: (0, 0, 0)),
            weight,
            weight,
            weight,
            pl.BlockSpec((8, TOK, TILE), lambda n: (0, 0, n)),
            line,
        ],
        out_specs=piece_specs() + (line,),
        compiler_params=params(),
        cost_estimate=cost(6e9, 20e6),
        name="inward",
    )(dqkv, wq, wk, wv, normed, gain)


def out_grad_kernel(sent, *rest):
    parts, out = rest[:10], rest[10]
    grads = rest[11]
    for k, (number, row, rows) in enumerate(WHERE):
        grads[number, row : row + rows] = parts[k][...]
    out[0] = tn(
        sent[...].reshape(8 * TOK, LOCAL), grads[...].reshape(8 * TOK, TILE)
    ).astype(BF16)


def out_grad(sent, parts):
    return pl.pallas_call(
        out_grad_kernel,
        grid=(D // TILE,),
        out_shape=jax.ShapeDtypeStruct((1, LOCAL, D), BF16),
        in_specs=[pl.BlockSpec((8, TOK, LOCAL), lambda n: (0, 0, 0))]
        + [pl.BlockSpec((rows, TILE), lambda n: (0, n)) for _, _, rows in WHERE],
        out_specs=pl.BlockSpec((1, LOCAL, TILE), lambda n: (0, 0, n)),
        scratch_shapes=[pltpu.VMEM((8, TOK, TILE), BF16)],
        compiler_params=params(),
        cost_estimate=cost(2e9, 8e6),
        name="out_grad",
    )(sent, *parts)


def weight_grad_kernel(normed, dqkv, gq, gk, gv):
    rows = normed[...].reshape(8 * TOK, TILE)
    flat = dqkv[...].reshape(8 * TOK, 3 * LOCAL)
    total = tn(rows, flat).astype(BF16)
    gq[0] = total[:, :LOCAL]
    gk[0] = total[:, LOCAL : 2 * LOCAL]
    gv[0] = total[:, 2 * LOCAL :]


def weight_grad(normed, dqkv):
    out = pl.BlockSpec((1, TILE, LOCAL), lambda n: (0, n, 0))
    return pl.pallas_call(
        weight_grad_kernel,
        grid=(D // TILE,),
        out_shape=(jax.ShapeDtypeStruct((1, D, LOCAL), BF16),) * 3,
        in_specs=[
            pl.BlockSpec((8, TOK, TILE), lambda n: (0, 0, n)),
            pl.BlockSpec((8, TOK, 3 * LOCAL), lambda n: (0, 0, 0)),
        ],
        out_specs=(out,) * 3,
        compiler_params=params(),
        cost_estimate=cost(6e9, 14e6),
        name="weight_grad",
    )(normed, dqkv)


def add(a, b):
    return (a.astype(F32) + b.astype(F32)).astype(BF16)


def ring_sum(u_up, u_down, v_up, v_down, k_up, k_down):
    got_up = moved(u_up, 0, 0, 1)
    got_down = moved(u_down, 0, 0, -1)
    high_a = moved(v_up, 0, 0, 1)
    low_a = moved(v_down, 0, 0, -1)
    low_b = moved(add(k_up, got_up), 0, 0, 1)
    high_b = moved(add(k_down, got_down), 0, 0, -1)
    return low_a, low_b, high_a, high_b


def summed(own, low_a, low_b, high_a, high_b, dx):
    low = own[dx, :HALF].astype(F32) + low_a[dx].astype(F32) + low_b[dx].astype(F32)
    high = own[dx, HALF:].astype(F32) + high_a[dx].astype(F32) + high_b[dx].astype(F32)
    return low, high


def end_forward_kernel(own, low_a, low_b, high_a, high_b, same, other):
    for dx, out in enumerate((same, other)):
        low, high = summed(own, low_a, low_b, high_a, high_b, dx)
        out[:HALF] = low.astype(BF16)
        out[HALF:] = high.astype(BF16)


def end_forward(*pieces):
    return pl.pallas_call(
        end_forward_kernel,
        out_shape=(jax.ShapeDtypeStruct((TOK, D), BF16),) * 2,
        in_specs=[VMEM] * 5,
        out_specs=(VMEM, VMEM),
        compiler_params=params(),
        cost_estimate=cost(1e6, 4e6),
        name="end_forward",
    )(*pieces)


def end_back_kernel(sigma, gain, enter_same, enter_other, own, low_a, low_b, high_a, high_b, *rest):
    parts = rest[:10]
    same, other, d_out, sems = rest[10:]
    wanted = jnp.int32(0)
    for r in range(8):
        wanted = wanted + jnp.where(sigma[r] == 0, r, 0)
    load_one(parts, wanted, d_out, sems)
    gain_row = gain[...].astype(F32)
    for dx, (enter, out) in enumerate(((enter_same, same), (enter_other, other))):
        halves = summed(own, low_a, low_b, high_a, high_b, dx)
        for start, d_normed in zip((0, HALF), halves, strict=True):
            rows = slice(start, start + HALF)
            act = enter[rows].astype(F32)
            inv_rms = lax.rsqrt(jnp.mean(act * act, axis=-1, keepdims=True) + eps)
            unit = act * inv_rms
            scaled = d_normed * gain_row
            d_act = inv_rms * (scaled - unit * jnp.mean(scaled * unit, axis=-1, keepdims=True))
            if dx == 0:
                d_act = d_act + d_out[rows].astype(F32)
            out[rows] = d_act.astype(BF16)


def end_back(sigma, gain, enter_same, enter_other, pieces, parts):
    return pl.pallas_call(
        end_back_kernel,
        out_shape=(jax.ShapeDtypeStruct((TOK, D), BF16),) * 2,
        in_specs=[SMEM] + [VMEM] * 8 + [ANY] * 10,
        out_specs=(VMEM, VMEM),
        scratch_shapes=[pltpu.VMEM((TOK, D), BF16), pltpu.SemaphoreType.DMA((10,))],
        compiler_params=params(),
        cost_estimate=cost(1e6, 6e6),
        name="end_back",
    )(sigma, gain, enter_same, enter_other, *pieces, *parts)


def sum_over_peers(value):
    value = value + moved(value, 0, 1, 0)
    pairs = [
        ((s * 2 + x) * RING + z, (s * 2 + x) * RING + (z ^ 1))
        for s in range(SECTIONS)
        for x in range(2)
        for z in range(RING)
    ]
    value = value + lax.ppermute(value, ("section", "peer"), pairs)
    return value + moved(value, 0, 0, 2)


def per_device(inputs, wiring, lengths, norm_gain, w_query, w_key, w_value, w_out, cotangent):
    peer = lax.axis_index("peer")
    ids = jnp.stack([lax.axis_index("section"), peer // RING, peer % RING]).astype(jnp.int32)
    entering = gather_all(inputs[0, 0], 1)
    later = gather_all(cotangent[0, 0], -1)
    entering_parts = [part[0] for part in entering]
    later_parts = [part[0] for part in later]
    sigma, normed, qkv, probs, mixed = forward(
        ids, wiring, lengths, norm_gain, w_query, w_key, w_value, entering_parts
    )
    *cut, own, sent = outward(sigma, mixed, w_out, entering_parts)
    same, other = end_forward(own, *ring_sum(*cut))
    final_out = add(moved(same, 1, 0, 0), moved(other, 1, 1, 0))

    dqkv = back(sigma, w_out, qkv, probs, later_parts)
    *cut, own, gain_part = inward(dqkv, w_query, w_key, w_value, normed, norm_gain)
    w_out_grad = out_grad(sent, later_parts)
    w_query_grad, w_key_grad, w_value_grad = weight_grad(normed, dqkv)
    gain_grad = sum_over_peers(gain_part)
    same, other = end_back(
        sigma, norm_gain, entering_parts[0], entering_parts[1], (own, *ring_sum(*cut)), later_parts
    )
    input_grad = add(moved(same, -1, 0, 0), moved(other, -1, 1, 0))
    return (
        final_out[None, None],
        input_grad[None, None],
        gain_grad,
        w_query_grad,
        w_key_grad,
        w_value_grad,
        w_out_grad,
    )


def solution(mesh):
    return jax.shard_map(
        per_device,
        mesh=mesh,
        in_specs=(
            P("section", "peer", None, None),
            P(),
            P(),
            P("section", None),
            P("section", None, "peer"),
            P("section", None, "peer"),
            P("section", None, "peer"),
            P("section", "peer", None),
            P("section", "peer", None, None),
        ),
        out_specs=(
            P("section", "peer", None, None),
            P("section", "peer", None, None),
            P("section", None),
            P("section", None, "peer"),
            P("section", None, "peer"),
            P("section", None, "peer"),
            P("section", "peer", None),
        ),
        check_vma=False,
    )
```

time: 582 us -> 288 us (0.49); the launches traced: 572 us -> 285 us
  waiting for transfers between devices: 353 us -> 110 us
  Pallas kernels: 0 us -> 86.3 us
  matrix products: 83.6 us -> 0 us
  starting transfers between devices: 6.77 us -> 72.9 us
  blocking collectives: 41.9 us -> 0 us
  other arithmetic: 35.2 us -> 6.09 us
  local copies, waits for them, and re-layouts: 35.7 us -> 8.62 us
  between operations: 16.3 us -> 0.99 us
    all_gather x2 -> x0, waiting for transfers between devices: 177 us -> none  [the longest x1 95 us: per_device(): grouped = lax.all_gather(inputs, 'peer', axis=1, tiled=True)]
    reduce_scatter x2 -> x0, waiting for transfers between devices: 135 us -> none  [the longest x1 85.7 us: per_device(): lax.psum_scatter(jnp.dot(mixed_sent, wo_local, preferred_element_type=jnp...]
    pallas_call x0 -> x8, Pallas kernels: none -> 86.3 us  [the longest x1 28.4 us: forward(): pl.pallas_call(forward_kernel, out_shape=(jax.ShapeDtypeStruct((8,), jnp....]
    dot_general x18 -> x0, matrix products: 83.6 us -> none  [the longest x3 16.6 us: project(): product = jnp.dot(normed, weight_mat, preferred_element_type=jnp.float32)]
    ppermute x4 -> x39, waiting for transfers between devices: 39.2 us -> 110 us  [the longest x38 110 us: moved(): return lax.ppermute(value, ('section', 'peer'), pairs)]
    ppermute x4 -> x39, starting transfers between devices: 6.61 us -> 72.9 us  [the longest x38 72.8 us: moved(): return lax.ppermute(value, ('section', 'peer'), pairs)]
    psum x1 -> x0, blocking collectives: 41.9 us -> none  [per_device(): gain_grad = lax.psum(gain_part, 'peer')]
    convert_element_type x3 -> x4, other arithmetic: 17.3 us -> 3.4 us  [add(): return (a.astype(F32) + b.astype(F32)).astype(BF16)]
  transfers between devices with their start and end apart: 8 -> 39, of which waited for: 5 -> 17; matrix products, arithmetic and copies ran while one was open for 13% -> 3% of each run, Pallas kernels for 0% -> 30%
where the time goes in v1:
time: 288 us; the launch traced here: 285 us
  waiting for transfers between devices  110 us (38%)
  Pallas kernels  86.3 us (30%)
  starting transfers between devices  72.9 us (25%)
  local copies, waits for them, and re-layouts  8.62 us (3%)
  other arithmetic  6.09 us (2%)
    ppermute x38, waiting for transfers between devices, moved(): return lax.ppermute(value, ('section', 'peer'), pairs)  110 us
    ppermute x38, starting transfers between devices, moved(): return lax.ppermute(value, ('section', 'peer'), pairs)  72.8 us
    pallas_call x1, Pallas kernels, forward(): pl.pallas_call(forward_kernel, out_shape=(jax.ShapeDtypeStruct((8,), jnp....  28.4 us
    pallas_call x1, Pallas kernels, back(): pl.pallas_call(back_kernel, out_shape=jax.ShapeDtypeStruct((8, TOK, 3 * L...  17.4 us
    pallas_call x1, Pallas kernels, inward(): pl.pallas_call(inward_kernel, grid=(D // TILE,), out_shape=piece_shapes()...  12.9 us
    pallas_call x1, Pallas kernels, weight_grad(): pl.pallas_call(weight_grad_kernel, grid=(D // TILE,), out_shape=(jax.Shap...  9.98 us
    pallas_call x1, Pallas kernels, outward(): pl.pallas_call(outward_kernel, grid=(D // TILE,), out_shape=piece_shapes(...  8.04 us
  transfers between devices with their start and end apart: 39, of which 17 were waited for; matrix products, arithmetic and copies ran while one was open for 3% of the time, Pallas kernels for 30%

profile of v1, /device:TPU:4, one launch (start us, length us, event | category | flops | bytes accessed | tf_op | source)
XLA Modules:
  0.0 284.6 jit_solution(7723050595450148463)
XLA Ops:
  0.7 4.3 %collective-permute-start.2 = (bf16[128,2560]{1,0:T(8,128)(2,1)}, bf16[128,2560]{1,0:T(8,128)(2,1)S(1)}, u32[]{:S(2)}, u32[]{:S(2)}) collective-permute-start(bf16[128,2560]{1,0:T(8,128)(2,1)} %bitcast.10), channel_id=1, source_target_pairs={{0,11},{1,8},{2,9},{3,10},{4,15},{5,12},{6,13},{7,14},{8,19},{9,16... | collective-permute-start | bytes 1966088 | tf_op jit(solution)/shard_map/ppermute | solution.py:35
  5.0 4.5 %collective-permute-start.19 = (bf16[128,2560]{1,0:T(8,128)(2,1)}, bf16[128,2560]{1,0:T(8,128)(2,1)S(1)}, u32[]{:S(2)}, u32[]{:S(2)}) collective-permute-start(bf16[128,2560]{1,0:T(8,128)(2,1)} %bitcast.13), channel_id=1, source_target_pairs={{0,124},{1,125},{2,126},{3,127},{4,120},{5,121},{6,122},{7,123},{8... | collective-permute-start | bytes 1966088 | tf_op jit(solution)/shard_map/ppermute | solution.py:35
  9.5 16.1 %collective-permute-done.1.rest_1_.enter_other = bf16[128,2560]{1,0:T(8,128)(2,1)S(1)} collective-permute-done((bf16[128,2560]{1,0:T(8,128)(2,1)}, bf16[128,2560]{1,0:T(8,128)(2,1)S(1)}, u32[]{:S(2)}, u32[]{:S(2)}) %collective-permute-start.1) | collective-permute-done | bytes 655392 | tf_op jit(solution)/shard_map/ppermute | solution.py:35
  25.7 3.9 %collective-permute-start.4 = (bf16[128,2560]{1,0:T(8,128)(2,1)S(1)}, bf16[128,2560]{1,0:T(8,128)(2,1)S(1)}, u32[]{:S(2)}, u32[]{:S(2)}) collective-permute-start(bf16[128,2560]{1,0:T(8,128)(2,1)S(1)} %collective-permute-done.1.rest_1_.enter_other), channel_id=1, source_target_pairs={{0,3},{1,0},{2,1},{3,2},{4,7},{5,4},{6,5},{7,6},{8,11},{9,8},{10,9... | collective-permute-start | bytes 1966088 | tf_op jit(solution)/shard_map/ppermute | solution.py:35
  33.6 4.2 %collective-permute-start.22 = (bf16[128,2560]{1,0:T(8,128)(2,1)S(1)}, bf16[128,2560]{1,0:T(8,128)(2,1)S(1)}, u32[]{:S(2)}, u32[]{:S(2)}) collective-permute-start(bf16[128,2560]{1,0:T(8,128)(2,1)S(1)} %collective-permute-done.19.rest_1_), channel_id=1, source_target_pairs={{0,3},{1,0},{2,1},{3,2},{4,7},{5,4},{6,5},{7,6},{8,11},{9,8},{10,9... | collective-permute-start | bytes 1966088 | tf_op jit(solution)/shard_map/ppermute | solution.py:35
  37.8 12.2 %collective-permute-done.4.rest_4_ = bf16[128,2560]{1,0:T(8,128)(2,1)S(1)} collective-permute-done((bf16[128,2560]{1,0:T(8,128)(2,1)S(1)}, bf16[128,2560]{1,0:T(8,128)(2,1)S(1)}, u32[]{:S(2)}, u32[]{:S(2)}) %collective-permute-start.4) | collective-permute-done | bytes 655392 | tf_op jit(solution)/shard_map/ppermute | solution.py:35
  50.0 5.4 %collective-permute-done.5.rest_5_ = bf16[128,2560]{1,0:T(8,128)(2,1)S(1)} collective-permute-done((bf16[128,2560]{1,0:T(8,128)(2,1)S(1)}, bf16[128,2560]{1,0:T(8,128)(2,1)S(1)}, u32[]{:S(2)}, u32[]{:S(2)}) %collective-permute-start.5) | collective-permute-done | bytes 655392 | tf_op jit(solution)/shard_map/ppermute | solution.py:35
  59.3 3.9 %collective-permute-done.21.rest_3_ = bf16[128,2560]{1,0:T(8,128)(2,1)S(1)} collective-permute-done((bf16[128,2560]{1,0:T(8,128)(2,1)}, bf16[128,2560]{1,0:T(8,128)(2,1)S(1)}, u32[]{:S(2)}, u32[]{:S(2)}) %collective-permute-start.21) | collective-permute-done | bytes 655392 | tf_op jit(solution)/shard_map/ppermute | solution.py:35
  66.4 3.1 %collective-permute-done.23.rest_5_ = bf16[128,2560]{1,0:T(8,128)(2,1)S(1)} collective-permute-done((bf16[128,2560]{1,0:T(8,128)(2,1)S(1)}, bf16[128,2560]{1,0:T(8,128)(2,1)S(1)}, u32[]{:S(2)}, u32[]{:S(2)}) %collective-permute-start.23) | collective-permute-done | bytes 655392 | tf_op jit(solution)/shard_map/ppermute | solution.py:35
  71.8 4.7 %collective-permute-start.18 = (bf16[128,2560]{1,0:T(8,128)(2,1)}, bf16[128,2560]{1,0:T(8,128)(2,1)S(1)}, u32[]{:S(2)}, u32[]{:S(2)}) collective-permute-start(bf16[128,2560]{1,0:T(8,128)(2,1)} %bitcast.16), channel_id=1, source_target_pairs={{0,120},{1,121},{2,122},{3,123},{4,124},{5,125},{6,126},{7,127},{8... | collective-permute-start | bytes 1966088 | tf_op jit(solution)/shard_map/ppermute | solution.py:35
  76.6 3.2 %collective-permute-start.25 = (bf16[64,2560]{1,0:T(8,128)(2,1)S(1)}, bf16[64,2560]{1,0:T(8,128)(2,1)S(1)}, u32[]{:S(2)}, u32[]{:S(2)}) collective-permute-start(bf16[64,2560]{1,0:T(8,128)(2,1)S(1)} %slice.37), channel_id=1, source_target_pairs={{0,3},{1,0},{2,1},{3,2},{4,7},{5,4},{6,5},{7,6},{8,11},{9,8},{10,9... | collective-permute-start | bytes 983048 | tf_op jit(solution)/shard_map/ppermute | solution.py:35
  79.9 3.8 %collective-permute-done.8.rest_8_ = bf16[64,2560]{1,0:T(8,128)(2,1)} collective-permute-done((bf16[64,2560]{1,0:T(8,128)(2,1)}, bf16[64,2560]{1,0:T(8,128)(2,1)}, u32[]{:S(2)}, u32[]{:S(2)}) %collective-permute-start.8) | collective-permute-done | bytes 327712 | tf_op jit(solution)/shard_map/ppermute | solution.py:35
  83.7 3.2 %collective-permute-start.27 = (bf16[64,2560]{1,0:T(8,128)(2,1)S(1)}, bf16[64,2560]{1,0:T(8,128)(2,1)S(1)}, u32[]{:S(2)}, u32[]{:S(2)}) collective-permute-start(bf16[64,2560]{1,0:T(8,128)(2,1)S(1)} %slice.39), channel_id=1, source_target_pairs={{0,3},{1,0},{2,1},{3,2},{4,7},{5,4},{6,5},{7,6},{8,11},{9,8},{10,9... | collective-permute-start | bytes 983048 | tf_op jit(solution)/shard_map/ppermute | solution.py:35
  88.0 28.4 %forward.1 = (s32[8]{0:T(128)S(1)}, bf16[8,128,2560]{2,1,0:T(8,128)(2,1)}, bf16[8,128,1152]{2,1,0:T(8,128)(2,1)}, f32[8,3,128,128]{3,2,1,0:T(8,128)}, bf16[8,128,384]{2,1,0:T(8,128)(2,1)S(1)}) custom-call(s32[3]{0:T(128)S(1)} %pad_add_fusion.ids, s32[2,16,8]{2,1,0:T(8,128)S(1)} %copy.16.wiring, s32[16,8]{1,0:T(8,128)S(1)} %copy.17.lengths, ...), custom_call_target="tpu_custom_call" | custom-call | flops 6300000256 | bytes 20000000 | tf_op jit(solution)/shard_map/forward/pallas_call | solution.py:169
  117.3 8.0 %outward.1 = (bf16[2,64,2560]{2,1,0:T(8,128)(2,1)S(1)}, bf16[2,64,2560]{2,1,0:T(8,128)(2,1)S(1)}, bf16[2,64,2560]{2,1,0:T(8,128)(2,1)S(1)}, bf16[2,64,2560]{2,1,...) custom-call(s32[8]{0:T(128)S(1)} %get-tuple-element.35.sigma, ...), custom_call_target="tpu_custom_call" | custom-call | flops 2000000000 | bytes 9000000 | tf_op jit(solution)/shard_map/outward/pallas_call | solution.py:235
  125.5 17.4 %back.1.dqkv = bf16[8,128,1152]{2,1,0:T(8,128)(2,1)} custom-call(s32[8]{0:T(128)S(1)} %get-tuple-element.35.sigma, bf16[1,384,2560]{2,1,0:T(8,128)(2,1)} %wo.3, bf16[8,128,1152]{2,1,0:T(8,128)(2,1)} %get-tuple-element.46.qkv, f32[8,3,128,128]{3,2,1,0:T(8,128)} %get-tuple-element.47.probs, bf16[128,2560]{1,0:T(8,128)(2,1)S(1)} %collective-permute-done.18.rest_0_, ...), custom_call_target="tpu_custom_call" | custom-call | flops 3000000000 | bytes 14000000 | tf_op jit(solution)/shard_map/back/pallas_call | solution.py:281
  142.9 12.9 %inward.1 = (bf16[2,64,2560]{2,1,0:T(8,128)(2,1)S(1)}, bf16[2,64,2560]{2,1,0:T(8,128)(2,1)S(1)}, bf16[2,64,2560]{2,1,0:T(8,128)(2,1)}, bf16[2,64,2560]{2,1,0:T(8...) custom-call(bf16[8,128,1152]{2,1,0:T(8,128)(2,1)} %back.1.dqkv, ...), custom_call_target="tpu_custom_call" | custom-call | flops 6000000000 | bytes 20000000 | tf_op jit(solution)/shard_map/inward/pallas_call | solution.py:311
  156.6 4.0 %collective-permute-start.36 = (f32[1,2560]{1,0:T(1,128)S(1)}, f32[1,2560]{1,0:T(1,128)S(1)}, u32[]{:S(2)}, u32[]{:S(2)}) collective-permute-start(f32[1,2560]{1,0:T(1,128)S(1)} %get-tuple-element.58), channel_id=1, source_target_pairs={{0,4},{1,5},{2,6},{3,7},{4,0},{5,1},{6,2},{7,3},{8,12},{9,13},{10,... | collective-permute-start | bytes 30728 | tf_op jit(solution)/shard_map/ppermute | solution.py:35
  162.4 3.2 %collective-permute-start.10 = (bf16[2,64,2560]{2,1,0:T(8,128)(2,1)S(1)}, bf16[2,64,2560]{2,1,0:T(8,128)(2,1)S(1)}, u32[]{:S(2)}, u32[]{:S(2)}) collective-permute-start(bf16[2,64,2560]{2,1,0:T(8,128)(2,1)S(1)} %get-tuple-element.38), channel_id=1, source_target_pairs={{0,3},{1,0},{2,1},{3,2},{4,7},{5,4},{6,5},{7,6},{8,11},{9,8},{10,9... | collective-permute-start | bytes 1966088 | tf_op jit(solution)/shard_map/ppermute | solution.py:35
  165.5 3.2 %collective-permute-start.14 = (bf16[2,64,2560]{2,1,0:T(8,128)(2,1)S(1)}, bf16[2,64,2560]{2,1,0:T(8,128)(2,1)S(1)}, u32[]{:S(2)}, u32[]{:S(2)}) collective-permute-start(bf16[2,64,2560]{2,1,0:T(8,128)(2,1)S(1)} %get-tuple-element.43), channel_id=1, source_target_pairs={{0,3},{1,0},{2,1},{3,2},{4,7},{5,4},{6,5},{7,6},{8,11},{9,8},{10,9... | collective-permute-start | bytes 1966088 | tf_op jit(solution)/shard_map/ppermute | solution.py:35
  172.1 16.2 %collective-permute-done.14 = bf16[2,64,2560]{2,1,0:T(8,128)(2,1)S(1)} collective-permute-done((bf16[2,64,2560]{2,1,0:T(8,128)(2,1)S(1)}, bf16[2,64,2560]{2,1,0:T(8,128)(2,1)S(1)}, u32[]{:S(2)}, u32[]{:S(2)}) %collective-permute-start.14) | collective-permute-done | bytes 655392 | tf_op jit(solution)/shard_map/ppermute | solution.py:35
  188.4 3.7 %collective-permute-start.32 = (bf16[2,64,2560]{2,1,0:T(8,128)(2,1)S(1)}, bf16[2,64,2560]{2,1,0:T(8,128)(2,1)S(1)}, u32[]{:S(2)}, u32[]{:S(2)}) collective-permute-start(bf16[2,64,2560]{2,1,0:T(8,128)(2,1)S(1)} %copy-done.24), channel_id=1, source_target_pairs={{0,3},{1,0},{2,1},{3,2},{4,7},{5,4},{6,5},{7,6},{8,11},{9,8},{10,9... | collective-permute-start | bytes 1966088 | tf_op jit(solution)/shard_map/ppermute | solution.py:35
  195.4 21.1 %collective-permute-done.32 = bf16[2,64,2560]{2,1,0:T(8,128)(2,1)S(1)} collective-permute-done((bf16[2,64,2560]{2,1,0:T(8,128)(2,1)S(1)}, bf16[2,64,2560]{2,1,0:T(8,128)(2,1)S(1)}, u32[]{:S(2)}, u32[]{:S(2)}) %collective-permute-start.32) | collective-permute-done | bytes 655392 | tf_op jit(solution)/shard_map/ppermute | solution.py:35
  216.6 3.7 %collective-permute-start.15 = (bf16[2,64,2560]{2,1,0:T(8,128)(2,1)S(1)}, bf16[2,64,2560]{2,1,0:T(8,128)(2,1)S(1)}, u32[]{:S(2)}, u32[]{:S(2)}) collective-permute-start(bf16[2,64,2560]{2,1,0:T(8,128)(2,1)S(1)} %add_convert_fusion.4), channel_id=1, source_target_pairs={{0,3},{1,0},{2,1},{3,2},{4,7},{5,4},{6,5},{7,6},{8,11},{9,8},{10,9... | collective-permute-start | bytes 1966088 | tf_op jit(solution)/shard_map/ppermute | solution.py:35
  221.8 9.8 %collective-permute-done.15.high_b = bf16[2,64,2560]{2,1,0:T(8,128)(2,1)S(1)} collective-permute-done((bf16[2,64,2560]{2,1,0:T(8,128)(2,1)S(1)}, bf16[2,64,2560]{2,1,0:T(8,128)(2,1)S(1)}, u32[]{:S(2)}, u32[]{:S(2)}) %collective-permute-start.15) | collective-permute-done | bytes 655392 | tf_op jit(solution)/shard_map/ppermute | solution.py:35
  231.6 3.7 %collective-permute-start.33 = (bf16[2,64,2560]{2,1,0:T(8,128)(2,1)}, bf16[2,64,2560]{2,1,0:T(8,128)(2,1)S(1)}, u32[]{:S(2)}, u32[]{:S(2)}) collective-permute-start(bf16[2,64,2560]{2,1,0:T(8,128)(2,1)} %add_convert_fusion.1), channel_id=1, source_target_pairs={{0,3},{1,0},{2,1},{3,2},{4,7},{5,4},{6,5},{7,6},{8,11},{9,8},{10,9... | collective-permute-start | bytes 1966088 | tf_op jit(solution)/shard_map/ppermute | solution.py:35
  235.8 8.4 %collective-permute-start.17 = (bf16[128,2560]{1,0:T(8,128)(2,1)S(1)}, bf16[128,2560]{1,0:T(8,128)(2,1)S(1)}, u32[]{:S(2)}, u32[]{:S(2)}) collective-permute-start(bf16[128,2560]{1,0:T(8,128)(2,1)S(1)} %get-tuple-element.45), channel_id=1, source_target_pairs={{0,12},{1,13},{2,14},{3,15},{4,8},{5,9},{6,10},{7,11},{8,20},{9,21... | collective-permute-start | bytes 1966088 | tf_op jit(solution)/shard_map/ppermute | solution.py:35
  244.2 4.4 %out_grad.1 = bf16[1,384,2560]{2,1,0:T(8,128)(2,1)} custom-call(bf16[8,128,384]{2,1,0:T(8,128)(2,1)S(1)} %copy-done.20, bf16[128,2560]{1,0:T(8,128)(2,1)S(1)} %collective-permute-done.18.rest_0_, bf16[128,2560]{1,0:T(8,128)(2,1)S(1)} %collective-permute-done.19.rest_1_, bf16[128,2560]{1,0:T(8,128)(2,1)S(1)} %collective-permute-done.20.rest_2_, ...), custom_call_target="tpu_custom_call" | custom-call | flops 2000000000 | bytes 8000000 | tf_op jit(solution)/shard_map/out_grad/pallas_call | solution.py:341
  248.6 10.0 %weight_grad.1 = (bf16[1,2560,384]{2,1,0:T(8,128)(2,1)}, bf16[1,2560,384]{2,1,0:T(8,128)(2,1)}, bf16[1,2560,384]{2,1,0:T(8,128)(2,1)}) custom-call(bf16[8,128,2560]{2,1,0:T(8,128)(2,1)} %get-tuple-element.48.normed, bf16[8,128,1152]{2,1,0:T(8,128)(2,1)S(1)} %copy-done.9), custom_call_target="tpu_custom_call" | custom-call | flops 6000000000 | bytes 14000000 | tf_op jit(solution)/shard_map/weight_grad/pallas_call | solution.py:366
  260.0 4.8 %end_back.1 = (bf16[128,2560]{1,0:T(8,128)(2,1)S(1)}, bf16[128,2560]{1,0:T(8,128)(2,1)S(1)}) custom-call(s32[8]{0:T(128)S(1)} %get-tuple-element.35.sigma, bf16[1,2560]{1,0:T(2,128)(2,1)S(1)} %copy-done.22, bf16[128,2560]{1,0:T(8,128)(2,1)} %collective-permute-done.rest_0_.enter_same, bf16[128,2560]{1,0:T(8,128)(2,1)S(1)} %copy-done.8, ...), custom_call_target="tpu_custom_call" | custom-call | flops 1000000 | bytes 6000000 | tf_op jit(solution)/shard_map/end_back/pallas_call | solution.py:443
  264.9 3.0 %collective-permute-start.35 = (bf16[128,2560]{1,0:T(8,128)(2,1)S(1)}, bf16[128,2560]{1,0:T(8,128)(2,1)S(1)}, u32[]{:S(2)}, u32[]{:S(2)}) collective-permute-start(bf16[128,2560]{1,0:T(8,128)(2,1)S(1)} %get-tuple-element.57), channel_id=1, source_target_pairs={{0,124},{1,125},{2,126},{3,127},{4,120},{5,121},{6,122},{7,123},{8... | collective-permute-start | bytes 1966088 | tf_op jit(solution)/shard_map/ppermute | solution.py:35
  270.3 11.8 %collective-permute-done.35 = bf16[128,2560]{1,0:T(8,128)(2,1)S(1)} collective-permute-done((bf16[128,2560]{1,0:T(8,128)(2,1)S(1)}, bf16[128,2560]{1,0:T(8,128)(2,1)S(1)}, u32[]{:S(2)}, u32[]{:S(2)}) %collective-permute-start.35) | collective-permute-done | bytes 655392 | tf_op jit(solution)/shard_map/ppermute | solution.py:35
  (130 shorter events, 33.2 us)
Async XLA Ops:
  0.6 25.1 %collective-permute-start.1 = (bf16[128,2560]{1,0:T(8,128)(2,1)}, bf16[128,2560]{1,0:T(8,128)(2,1)S(1)}, u32[]{:S(2)}, u32[]{:S(2)}) collective-permute-start(bf16[128,2560]{1,0:T(8,128)(2,1)} %bitcast.9), channel_id=1, source_target_pairs={{0,12},{1,13},{2,14},{3,15},{4,8},{5,9},{6,10},{7,11},{8,20},{9,21... | collective-permute-start | bytes 1966088 | tf_op jit(solution)/shard_map/ppermute | solution.py:35
  0.7 29.7 %collective-permute-start.2 = (bf16[128,2560]{1,0:T(8,128)(2,1)}, bf16[128,2560]{1,0:T(8,128)(2,1)S(1)}, u32[]{:S(2)}, u32[]{:S(2)}) collective-permute-start(bf16[128,2560]{1,0:T(8,128)(2,1)} %bitcast.10), channel_id=1, source_target_pairs={{0,11},{1,8},{2,9},{3,10},{4,15},{5,12},{6,13},{7,14},{8,19},{9,16... | collective-permute-start | bytes 1966088 | tf_op jit(solution)/shard_map/ppermute | solution.py:35
  5.0 27.2 %collective-permute-start.3 = (bf16[128,2560]{1,0:T(8,128)(2,1)}, bf16[128,2560]{1,0:T(8,128)(2,1)S(1)}, u32[]{:S(2)}, u32[]{:S(2)}) collective-permute-start(bf16[128,2560]{1,0:T(8,128)(2,1)} %bitcast.11), channel_id=1, source_target_pairs={{0,9},{1,10},{2,11},{3,8},{4,13},{5,14},{6,15},{7,12},{8,17},{9,18... | collective-permute-start | bytes 1966088 | tf_op jit(solution)/shard_map/ppermute | solution.py:35
  5.0 28.6 %collective-permute-start.19 = (bf16[128,2560]{1,0:T(8,128)(2,1)}, bf16[128,2560]{1,0:T(8,128)(2,1)S(1)}, u32[]{:S(2)}, u32[]{:S(2)}) collective-permute-start(bf16[128,2560]{1,0:T(8,128)(2,1)} %bitcast.13), channel_id=1, source_target_pairs={{0,124},{1,125},{2,126},{3,127},{4,120},{5,121},{6,122},{7,123},{8... | collective-permute-start | bytes 1966088 | tf_op jit(solution)/shard_map/ppermute | solution.py:35
  25.7 24.3 %collective-permute-start.4 = (bf16[128,2560]{1,0:T(8,128)(2,1)S(1)}, bf16[128,2560]{1,0:T(8,128)(2,1)S(1)}, u32[]{:S(2)}, u32[]{:S(2)}) collective-permute-start(bf16[128,2560]{1,0:T(8,128)(2,1)S(1)} %collective-permute-done.1.rest_1_.enter_other), channel_id=1, source_target_pairs={{0,3},{1,0},{2,1},{3,2},{4,7},{5,4},{6,5},{7,6},{8,11},{9,8},{10,9... | collective-permute-start | bytes 1966088 | tf_op jit(solution)/shard_map/ppermute | solution.py:35
  29.6 25.9 %collective-permute-start.5 = (bf16[128,2560]{1,0:T(8,128)(2,1)S(1)}, bf16[128,2560]{1,0:T(8,128)(2,1)S(1)}, u32[]{:S(2)}, u32[]{:S(2)}) collective-permute-start(bf16[128,2560]{1,0:T(8,128)(2,1)S(1)} %collective-permute-done.1.rest_1_.enter_other), channel_id=1, source_target_pairs={{0,1},{1,2},{2,3},{3,0},{4,5},{5,6},{6,7},{7,4},{8,9},{9,10},{10,1... | collective-permute-start | bytes 1966088 | tf_op jit(solution)/shard_map/ppermute | solution.py:35
  30.4 28.9 %collective-permute-start.20 = (bf16[128,2560]{1,0:T(8,128)(2,1)}, bf16[128,2560]{1,0:T(8,128)(2,1)S(1)}, u32[]{:S(2)}, u32[]{:S(2)}) collective-permute-start(bf16[128,2560]{1,0:T(8,128)(2,1)} %bitcast.14), channel_id=1, source_target_pairs={{0,123},{1,120},{2,121},{3,122},{4,127},{5,124},{6,125},{7,126},{8... | collective-permute-start | bytes 1966088 | tf_op jit(solution)/shard_map/ppermute | solution.py:35
  32.2 31.1 %collective-permute-start.21 = (bf16[128,2560]{1,0:T(8,128)(2,1)}, bf16[128,2560]{1,0:T(8,128)(2,1)S(1)}, u32[]{:S(2)}, u32[]{:S(2)}) collective-permute-start(bf16[128,2560]{1,0:T(8,128)(2,1)} %bitcast.15), channel_id=1, source_target_pairs={{0,121},{1,122},{2,123},{3,120},{4,125},{5,126},{6,127},{7,124},{8... | collective-permute-start | bytes 1966088 | tf_op jit(solution)/shard_map/ppermute | solution.py:35
  33.6 30.5 %collective-permute-start.22 = (bf16[128,2560]{1,0:T(8,128)(2,1)S(1)}, bf16[128,2560]{1,0:T(8,128)(2,1)S(1)}, u32[]{:S(2)}, u32[]{:S(2)}) collective-permute-start(bf16[128,2560]{1,0:T(8,128)(2,1)S(1)} %collective-permute-done.19.rest_1_), channel_id=1, source_target_pairs={{0,3},{1,0},{2,1},{3,2},{4,7},{5,4},{6,5},{7,6},{8,11},{9,8},{10,9... | collective-permute-start | bytes 1966088 | tf_op jit(solution)/shard_map/ppermute | solution.py:35
  50.0 19.5 %collective-permute-start.23 = (bf16[128,2560]{1,0:T(8,128)(2,1)S(1)}, bf16[128,2560]{1,0:T(8,128)(2,1)S(1)}, u32[]{:S(2)}, u32[]{:S(2)}) collective-permute-start(bf16[128,2560]{1,0:T(8,128)(2,1)S(1)} %collective-permute-done.19.rest_1_), channel_id=1, source_target_pairs={{0,1},{1,2},{2,3},{3,0},{4,5},{5,6},{6,7},{7,4},{8,9},{9,10},{10,1... | collective-permute-start | bytes 1966088 | tf_op jit(solution)/shard_map/ppermute | solution.py:35
  59.3 17.3 %collective-permute-start.6 = (bf16[64,2560]{1,0:T(8,128)(2,1)}, bf16[64,2560]{1,0:T(8,128)(2,1)}, u32[]{:S(2)}, u32[]{:S(2)}) collective-permute-start(bf16[64,2560]{1,0:T(8,128)(2,1)} %slice.32), channel_id=1, source_target_pairs={{0,1},{1,2},{2,3},{3,0},{4,5},{5,6},{6,7},{7,4},{8,9},{9,10},{10,1... | collective-permute-start | bytes 983048 | tf_op jit(solution)/shard_map/ppermute | solution.py:35
  64.1 19.6 %collective-permute-start.8 = (bf16[64,2560]{1,0:T(8,128)(2,1)}, bf16[64,2560]{1,0:T(8,128)(2,1)}, u32[]{:S(2)}, u32[]{:S(2)}) collective-permute-start(bf16[64,2560]{1,0:T(8,128)(2,1)} %slice.34), channel_id=1, source_target_pairs={{0,1},{1,2},{2,3},{3,0},{4,5},{5,6},{6,7},{7,4},{8,9},{9,10},{10,1... | collective-permute-start | bytes 983048 | tf_op jit(solution)/shard_map/ppermute | solution.py:35
  71.8 53.5 %collective-permute-start.18 = (bf16[128,2560]{1,0:T(8,128)(2,1)}, bf16[128,2560]{1,0:T(8,128)(2,1)S(1)}, u32[]{:S(2)}, u32[]{:S(2)}) collective-permute-start(bf16[128,2560]{1,0:T(8,128)(2,1)} %bitcast.16), channel_id=1, source_target_pairs={{0,120},{1,121},{2,122},{3,123},{4,124},{5,125},{6,126},{7,127},{8... | collective-permute-start | bytes 1966088 | tf_op jit(solution)/shard_map/ppermute | solution.py:35
  76.6 48.8 %collective-permute-start.24 = (bf16[64,2560]{1,0:T(8,128)(2,1)S(1)}, bf16[64,2560]{1,0:T(8,128)(2,1)S(1)}, u32[]{:S(2)}, u32[]{:S(2)}) collective-permute-start(bf16[64,2560]{1,0:T(8,128)(2,1)S(1)} %slice.36), channel_id=1, source_target_pairs={{0,1},{1,2},{2,3},{3,0},{4,5},{5,6},{6,7},{7,4},{8,9},{9,10},{10,1... | collective-permute-start | bytes 983048 | tf_op jit(solution)/shard_map/ppermute | solution.py:35
  76.6 48.8 %collective-permute-start.25 = (bf16[64,2560]{1,0:T(8,128)(2,1)S(1)}, bf16[64,2560]{1,0:T(8,128)(2,1)S(1)}, u32[]{:S(2)}, u32[]{:S(2)}) collective-permute-start(bf16[64,2560]{1,0:T(8,128)(2,1)S(1)} %slice.37), channel_id=1, source_target_pairs={{0,3},{1,0},{2,1},{3,2},{4,7},{5,4},{6,5},{7,6},{8,11},{9,8},{10,9... | collective-permute-start | bytes 983048 | tf_op jit(solution)/shard_map/ppermute | solution.py:35
  83.7 41.8 %collective-permute-start.26 = (bf16[64,2560]{1,0:T(8,128)(2,1)S(1)}, bf16[64,2560]{1,0:T(8,128)(2,1)S(1)}, u32[]{:S(2)}, u32[]{:S(2)}) collective-permute-start(bf16[64,2560]{1,0:T(8,128)(2,1)S(1)} %slice.38), channel_id=1, source_target_pairs={{0,1},{1,2},{2,3},{3,0},{4,5},{5,6},{6,7},{7,4},{8,9},{9,10},{10,1... | collective-permute-start | bytes 983048 | tf_op jit(solution)/shard_map/ppermute | solution.py:35
  83.7 41.8 %collective-permute-start.27 = (bf16[64,2560]{1,0:T(8,128)(2,1)S(1)}, bf16[64,2560]{1,0:T(8,128)(2,1)S(1)}, u32[]{:S(2)}, u32[]{:S(2)}) collective-permute-start(bf16[64,2560]{1,0:T(8,128)(2,1)S(1)} %slice.39), channel_id=1, source_target_pairs={{0,3},{1,0},{2,1},{3,2},{4,7},{5,4},{6,5},{7,6},{8,11},{9,8},{10,9... | collective-permute-start | bytes 983048 | tf_op jit(solution)/shard_map/ppermute | solution.py:35
  125.3 44.2 %collective-permute-start.11 = (bf16[2,64,2560]{2,1,0:T(8,128)(2,1)S(1)}, bf16[2,64,2560]{2,1,0:T(8,128)(2,1)}, u32[]{:S(2)}, u32[]{:S(2)}) collective-permute-start(bf16[2,64,2560]{2,1,0:T(8,128)(2,1)S(1)} %get-tuple-element.40), channel_id=1, source_target_pairs={{0,1},{1,2},{2,3},{3,0},{4,5},{5,6},{6,7},{7,4},{8,9},{9,10},{10,1... | collective-permute-start | bytes 1966088 | tf_op jit(solution)/shard_map/ppermute | solution.py:35
  162.4 31.7 %collective-permute-start.10 = (bf16[2,64,2560]{2,1,0:T(8,128)(2,1)S(1)}, bf16[2,64,2560]{2,1,0:T(8,128)(2,1)S(1)}, u32[]{:S(2)}, u32[]{:S(2)}) collective-permute-start(bf16[2,64,2560]{2,1,0:T(8,128)(2,1)S(1)} %get-tuple-element.38), channel_id=1, source_target_pairs={{0,3},{1,0},{2,1},{3,2},{4,7},{5,4},{6,5},{7,6},{8,11},{9,8},{10,9... | collective-permute-start | bytes 1966088 | tf_op jit(solution)/shard_map/ppermute | solution.py:35
  165.5 55.7 %collective-permute-start.13 = (bf16[2,64,2560]{2,1,0:T(8,128)(2,1)S(1)}, bf16[2,64,2560]{2,1,0:T(8,128)(2,1)S(1)}, u32[]{:S(2)}, u32[]{:S(2)}) collective-permute-start(bf16[2,64,2560]{2,1,0:T(8,128)(2,1)S(1)} %get-tuple-element.41), channel_id=1, source_target_pairs={{0,1},{1,2},{2,3},{3,0},{4,5},{5,6},{6,7},{7,4},{8,9},{9,10},{10,1... | collective-permute-start | bytes 1966088 | tf_op jit(solution)/shard_map/ppermute | solution.py:35
  165.5 22.8 %collective-permute-start.14 = (bf16[2,64,2560]{2,1,0:T(8,128)(2,1)S(1)}, bf16[2,64,2560]{2,1,0:T(8,128)(2,1)S(1)}, u32[]{:S(2)}, u32[]{:S(2)}) collective-permute-start(bf16[2,64,2560]{2,1,0:T(8,128)(2,1)S(1)} %get-tuple-element.43), channel_id=1, source_target_pairs={{0,3},{1,0},{2,1},{3,2},{4,7},{5,4},{6,5},{7,6},{8,11},{9,8},{10,9... | collective-permute-start | bytes 1966088 | tf_op jit(solution)/shard_map/ppermute | solution.py:35
  168.8 75.4 %collective-permute-start.28 = (bf16[2,64,2560]{2,1,0:T(8,128)(2,1)S(1)}, bf16[2,64,2560]{2,1,0:T(8,128)(2,1)S(1)}, u32[]{:S(2)}, u32[]{:S(2)}) collective-permute-start(bf16[2,64,2560]{2,1,0:T(8,128)(2,1)S(1)} %get-tuple-element.50), channel_id=1, source_target_pairs={{0,3},{1,0},{2,1},{3,2},{4,7},{5,4},{6,5},{7,6},{8,11},{9,8},{10,9... | collective-permute-start | bytes 1966088 | tf_op jit(solution)/shard_map/ppermute | solution.py:35
  169.5 22.8 %collective-permute-start.29 = (bf16[2,64,2560]{2,1,0:T(8,128)(2,1)S(1)}, bf16[2,64,2560]{2,1,0:T(8,128)(2,1)S(1)}, u32[]{:S(2)}, u32[]{:S(2)}) collective-permute-start(bf16[2,64,2560]{2,1,0:T(8,128)(2,1)S(1)} %get-tuple-element.52), channel_id=1, source_target_pairs={{0,1},{1,2},{2,3},{3,0},{4,5},{5,6},{6,7},{7,4},{8,9},{9,10},{10,1... | collective-permute-start | bytes 1966088 | tf_op jit(solution)/shard_map/ppermute | solution.py:35
  188.4 28.2 %collective-permute-start.32 = (bf16[2,64,2560]{2,1,0:T(8,128)(2,1)S(1)}, bf16[2,64,2560]{2,1,0:T(8,128)(2,1)S(1)}, u32[]{:S(2)}, u32[]{:S(2)}) collective-permute-start(bf16[2,64,2560]{2,1,0:T(8,128)(2,1)S(1)} %copy-done.24), channel_id=1, source_target_pairs={{0,3},{1,0},{2,1},{3,2},{4,7},{5,4},{6,5},{7,6},{8,11},{9,8},{10,9... | collective-permute-start | bytes 1966088 | tf_op jit(solution)/shard_map/ppermute | solution.py:35
  192.3 43.4 %collective-permute-start.38 = (f32[1,2560]{1,0:T(1,128)S(1)}, f32[1,2560]{1,0:T(1,128)S(1)}, u32[]{:S(2)}, u32[]{:S(2)}) collective-permute-start(f32[1,2560]{1,0:T(1,128)S(1)} %add.40), channel_id=1, source_target_pairs={{0,2},{1,3},{2,0},{3,1},{4,6},{5,7},{6,4},{7,5},{8,10},{9,11},{10,... | collective-permute-start | bytes 30728 | tf_op jit(solution)/shard_map/ppermute | solution.py:35
  194.0 27.2 %collective-permute-start.12 = (bf16[2,64,2560]{2,1,0:T(8,128)(2,1)S(1)}, bf16[2,64,2560]{2,1,0:T(8,128)(2,1)S(1)}, u32[]{:S(2)}, u32[]{:S(2)}) collective-permute-start(bf16[2,64,2560]{2,1,0:T(8,128)(2,1)S(1)} %add_convert_fusion.5), channel_id=1, source_target_pairs={{0,1},{1,2},{2,3},{3,0},{4,5},{5,6},{6,7},{7,4},{8,9},{9,10},{10,1... | collective-permute-start | bytes 1966088 | tf_op jit(solution)/shard_map/ppermute | solution.py:35
  221.2 37.9 %collective-permute-start.31 = (bf16[2,64,2560]{2,1,0:T(8,128)(2,1)}, bf16[2,64,2560]{2,1,0:T(8,128)(2,1)S(1)}, u32[]{:S(2)}, u32[]{:S(2)}) collective-permute-start(bf16[2,64,2560]{2,1,0:T(8,128)(2,1)} %get-tuple-element.53), channel_id=1, source_target_pairs={{0,1},{1,2},{2,3},{3,0},{4,5},{5,6},{6,7},{7,4},{8,9},{9,10},{10,1... | collective-permute-start | bytes 1966088 | tf_op jit(solution)/shard_map/ppermute | solution.py:35
  221.2 37.9 %collective-permute-start.30 = (bf16[2,64,2560]{2,1,0:T(8,128)(2,1)}, bf16[2,64,2560]{2,1,0:T(8,128)(2,1)S(1)}, u32[]{:S(2)}, u32[]{:S(2)}) collective-permute-start(bf16[2,64,2560]{2,1,0:T(8,128)(2,1)} %add_convert_fusion.2), channel_id=1, source_target_pairs={{0,1},{1,2},{2,3},{3,0},{4,5},{5,6},{6,7},{7,4},{8,9},{9,10},{10,1... | collective-permute-start | bytes 1966088 | tf_op jit(solution)/shard_map/ppermute | solution.py:35
  231.6 27.6 %collective-permute-start.33 = (bf16[2,64,2560]{2,1,0:T(8,128)(2,1)}, bf16[2,64,2560]{2,1,0:T(8,128)(2,1)S(1)}, u32[]{:S(2)}, u32[]{:S(2)}) collective-permute-start(bf16[2,64,2560]{2,1,0:T(8,128)(2,1)} %add_convert_fusion.1), channel_id=1, source_target_pairs={{0,3},{1,0},{2,1},{3,2},{4,7},{5,4},{6,5},{7,6},{8,11},{9,8},{10,9... | collective-permute-start | bytes 1966088 | tf_op jit(solution)/shard_map/ppermute | solution.py:35
  235.8 33.6 %collective-permute-start.17 = (bf16[128,2560]{1,0:T(8,128)(2,1)S(1)}, bf16[128,2560]{1,0:T(8,128)(2,1)S(1)}, u32[]{:S(2)}, u32[]{:S(2)}) collective-permute-start(bf16[128,2560]{1,0:T(8,128)(2,1)S(1)} %get-tuple-element.45), channel_id=1, source_target_pairs={{0,12},{1,13},{2,14},{3,15},{4,8},{5,9},{6,10},{7,11},{8,20},{9,21... | collective-permute-start | bytes 1966088 | tf_op jit(solution)/shard_map/ppermute | solution.py:35
  244.1 25.2 %collective-permute-start.16 = (bf16[128,2560]{1,0:T(8,128)(2,1)S(1)}, bf16[128,2560]{1,0:T(8,128)(2,1)S(1)}, u32[]{:S(2)}, u32[]{:S(2)}) collective-permute-start(bf16[128,2560]{1,0:T(8,128)(2,1)S(1)} %get-tuple-element.44), channel_id=1, source_target_pairs={{0,8},{1,9},{2,10},{3,11},{4,12},{5,13},{6,14},{7,15},{8,16},{9,17... | collective-permute-start | bytes 1966088 | tf_op jit(solution)/shard_map/ppermute | solution.py:35
  264.9 17.3 %collective-permute-start.35 = (bf16[128,2560]{1,0:T(8,128)(2,1)S(1)}, bf16[128,2560]{1,0:T(8,128)(2,1)S(1)}, u32[]{:S(2)}, u32[]{:S(2)}) collective-permute-start(bf16[128,2560]{1,0:T(8,128)(2,1)S(1)} %get-tuple-element.57), channel_id=1, source_target_pairs={{0,124},{1,125},{2,126},{3,127},{4,120},{5,121},{6,122},{7,123},{8... | collective-permute-start | bytes 1966088 | tf_op jit(solution)/shard_map/ppermute | solution.py:35
  (35 other events, 1584.6 us)
